TPU v7x, 32 devices: a whole 2x2x4 slice. The times are simulated.
32 devices in a mesh: groups: 2 (over x), tx: 16 (over z, y, core).
Axes of the slice: x: 2, y: 2, z: 4, core: 2. Of those that a mesh axis runs over, the one named last changes fastest.
Arguments:
- features: bfloat16 [384, 64, 128], P(('groups', 'tx')), parts along dimension 0, may hold values from -6 to 6
- nbr_table: int32 [384, 27], P(('groups', 'tx')), parts along dimension 0, may hold values from 0 to 20, as said below
- rim_slots: int32 [32, 8], P(('groups', 'tx')), parts along dimension 0, may hold values from 0 to 12, as said below
- w_first: bfloat16 [3456, 128], P('tx'), may hold values from -0.1875 to 0.1875
- w_second: bfloat16 [3456, 128], P('tx'), may hold values from -0.1875 to 0.1875
- cotangent: bfloat16 [384, 64, 128], P(('groups', 'tx')), parts along dimension 0, may hold values from -0.059814453 to 0.059814453
Outputs:
- out_map: bfloat16 [384, 64, 128], P(('groups', 'tx')), parts along dimension 0
- grad_first: float32 [6912, 128], P(('groups', 'tx')), parts along dimension 0
- grad_second: float32 [6912, 128], P(('groups', 'tx')), parts along dimension 0
There are 2 independent parts, one for each index of `groups`. A program takes and returns all parts, laid end to end along the dimension named above; an argument that names none is the same for every part. Nothing has to cross between parts.
Inputs may be any that keep to these rules, and one draw needn't show every extreme that they name: `nbr_table`: A tile's bricks lie in 3 brick rows of 2 by 2 positions; the map strips of tiles t and t+1 touch at t's last and t+1's first brick row. Entry q of an active slot names the brick at brick offset q: a slot of the same tile (0 to 11), 12+i for entry i of the previous tile's last-row list, 12 + 4+i for entry i of the next tile's first-row list, or 20 where that brick is inactive or outside the map; every entry of an empty slot is 20. Some tiles have all 12 slots active. `rim_slots`: each half lists the active bricks of that brick row in order of position, then 12 up to 4 entries; every tile has at least one active brick in its first and in its last brick row, and some tiles have 4 in both.
All inputs are finite; a program needn't handle non-finite values.
Results may differ from a plain program's by a relative error of at most 0.0049.
Values may be sent and summed in bfloat16 or wider, within the bound.
A program may use at most 64 MiB of HBM per device.

v0:
```python
import jax
import jax.numpy as jnp
import numpy as np
from jax import lax
from jax.sharding import PartitionSpec as P

BS = 4


def padded_2(x, sides, width):
    for axis, dim in sides:
        size, length = (lax.axis_size(axis), x.shape[dim])
        up = [(i, (i + 1) % size) for i in range(size - 1)]
        down = [(j, i) for i, j in up]
        last = lax.slice_in_dim(x, length - width, length, axis=dim)
        initial = lax.slice_in_dim(x, 0, width, axis=dim)
        before = lax.ppermute(last, axis, up)
        after = lax.ppermute(initial, axis, down)
        x = jnp.concatenate([before, x, after], axis=dim)
    return x


def brick_tables(side):
    coords = np.arange(side**3)
    first = coords // (side * side)
    second = coords // side % side
    third = coords % side
    brick_code = np.zeros((side**3, 27), np.int32)
    voxel_code = np.zeros((side**3, 27), np.int32)
    for offset in range(27):
        shifts = (offset // 9 - 1, offset // 3 % 3 - 1, offset % 3 - 1)
        code = np.zeros(side**3, np.int32)
        local = np.zeros(side**3, np.int32)
        for along, step in zip((first, second, third), shifts):
            moved = along + step
            brick_step = moved // side
            code = code * 3 + brick_step + 1
            local = local * side + moved - brick_step * side
        brick_code[:, offset] = code
        voxel_code[:, offset] = local
    return (brick_code, voxel_code)


def windows(extended, table, brick_code, voxel_code):
    vox_count = extended.shape[1]
    flat = extended.reshape(-1, extended.shape[2])
    index = table[:, brick_code] * vox_count + jnp.asarray(voxel_code)[None]
    picked = jnp.take(flat, index.reshape(-1).astype(jnp.int32), axis=0)
    return picked.reshape(table.shape[0] * vox_count, -1)


def on_device(features, nbr_table, rim_slots, w_first, w_second, cotangent):
    capacity, vox_count, channels = features.shape
    rim_count = rim_slots.shape[1] // 2
    brick_code, voxel_code = brick_tables(BS)
    zero_brick = jnp.zeros((1, vox_count, channels), jnp.bfloat16)
    own_lists = rim_slots[0]

    def extend(blocks):
        padded = jnp.concatenate([blocks, zero_brick], axis=0)
        packed = jnp.take(padded, own_lists, axis=0)
        beside_all = padded_2(packed, (("tx", 0),), rim_count)
        return jnp.concatenate(
            [blocks, beside_all[:rim_count], beside_all[3 * rim_count :], zero_brick], axis=0
        )

    inputs = windows(extend(features), nbr_table, brick_code, voxel_code)
    piece = lax.all_gather(w_first, "tx", axis=0, tiled=True)
    column_block = lax.slice_in_dim(inputs, 0, piece.shape[0], axis=1)
    first_sum = jnp.dot(column_block, piece, preferred_element_type=jnp.float32)
    hidden = jax.nn.silu(first_sum).astype(jnp.bfloat16)
    second_whole = lax.all_gather(w_second, "tx", axis=0, tiled=True)
    middle = windows(
        extend(hidden.reshape(capacity, vox_count, channels)), nbr_table, brick_code, voxel_code
    )
    out_map = jnp.dot(middle, second_whole, preferred_element_type=jnp.float32).astype(jnp.bfloat16)
    out_map = out_map.reshape(capacity, vox_count, channels)
    cot_rows = cotangent.reshape(-1, channels)
    contract = (((0,), (0,)), ((), ()))
    kernel_count = second_whole.shape[0] // channels
    flipped = (
        second_whole.reshape(kernel_count, channels, channels)[::-1]
        .transpose(0, 2, 1)
        .reshape(-1, channels)
    )
    back = jnp.dot(
        windows(extend(cotangent), nbr_table, brick_code, voxel_code),
        flipped,
        preferred_element_type=jnp.float32,
    )
    sigmoid_mid = jax.nn.sigmoid(first_sum)
    grad_mid = (back * sigmoid_mid * (1.0 + first_sum * (1.0 - sigmoid_mid))).astype(jnp.bfloat16)
    term_second = lax.dot_general(middle, cot_rows, contract, preferred_element_type=jnp.float32)
    term_first = lax.dot_general(inputs, grad_mid, contract, preferred_element_type=jnp.float32)
    grad_first, grad_second = (
        lax.psum_scatter(term_first, "tx", scatter_dimension=0, tiled=True),
        lax.psum_scatter(term_second, "tx", scatter_dimension=0, tiled=True),
    )
    return (out_map, grad_first, grad_second)


def solution(mesh):
    placed = (
        P(("groups", "tx"), None, None),
        P(("groups", "tx"), None),
        P(("groups", "tx"), None),
        P("tx", None),
        P("tx", None),
        P(("groups", "tx"), None, None),
    )
    return jax.shard_map(
        on_device,
        mesh=mesh,
        in_specs=placed,
        out_specs=(
            P(("groups", "tx"), None, None),
            P(("groups", "tx"), None),
            P(("groups", "tx"), None),
        ),
        check_vma=False,
    )
```

profile of v0, /device:TPU:0, one launch (start us, length us, event | category | flops | bytes accessed | tf_op | source)
XLA Modules:
  0.0 361.7 jit_solution(17203760057079737006)
XLA Ops:
  7.2 0.7 compare_select_fusion.1
  7.9 0.7 compare_and_fusion.1
  8.6 0.9 concatenate.22
  9.5 0.9 concatenate.18
  11.7 0.7 fusion.10
  12.4 3.0 collective-permute-start
  15.4 1.3 collective-permute-start.1
  16.6 0.7 fusion.8
  17.3 5.2 %collective-permute-start.4 = (bf16[4,64,128]{2,1,0:T(8,128)(2,1)}, bf16[4,64,128]{2,1,0:T(8,128)(2,1)}, u32[]{:S(2)}, u32[]{:S(2)}) collective-permute-start(bf16[4,64,128]{2,1,0:T(8,128)(2,1)} %get-tuple-element.5), channel_id=1, source_target_pairs={{0,1},{1,2},{2,3},{3,4},{4,5},{5,6},{6,7},{7,8},{8,9},{9,10},{10,1... | collective-permute-start | bytes 196616 | tf_op jit(solution)/shard_map/ppermute | solution.py:17
  22.5 1.3 collective-permute-start.5
  23.8 0.8 copy.23
  24.6 0.7 pad_clamp_fusion.1
  25.3 3.3 gather_fusion
  30.9 27.3 %all_gather.6 = bf16[3456,128]{1,0:T(8,128)(2,1)} all-gather(bf16[216,128]{1,0:T(8,128)(2,1)S(1)} %copy-done.3), channel_id=1, replica_groups=mesh['groups'=2,'tx'=16] {'tx'}, dimensions={0}, use_global_device_ids=true | all-gather | bytes 940032 | tf_op jit(solution)/shard_map/all_gather | solution.py:68
  58.2 19.9 %all_gather.7 = bf16[3456,128]{1,0:T(8,128)(2,1)S(1)} all-gather(bf16[216,128]{1,0:T(8,128)(2,1)S(1)} %copy-done.4), channel_id=1, replica_groups=mesh['groups'=2,'tx'=16] {'tx'}, dimensions={0}, use_global_device_ids=true | all-gather | bytes 940032 | tf_op jit(solution)/shard_map/all_gather | solution.py:72
  78.2 1.3 copy.25
  79.6 1.2 maximum_maximum_fusion.2
  80.8 45.9 %gather_fusion.6 = bf16[20736,128]{1,0:T(8,128)(2,1)} fusion(bf16[1344,128]{1,0:T(8,128)(2,1)S(1)} %bitcast.30, s32[21504]{0:T(1024)} %pad_clamp_fusion), kind=kCustom, calls=%fused_computation.5.clone | custom fusion | bytes 10699776 | tf_op jit(solution)/shard_map/jit(_take)/gather | solution.py:48
  126.8 42.0 %gather_fusion.2 = bf16[20736,128]{1,0:T(8,128)(2,1)} fusion(bf16[1344,128]{1,0:T(8,128)(2,1)S(1)} %bitcast.29, s32[21504]{0:T(1024)S(1)} %copy-done.1), kind=kCustom, calls=%fused_computation.1.clone | custom fusion | bytes 10699776 | tf_op jit(solution)/shard_map/jit(_take)/gather | solution.py:48
  168.8 12.7 %broadcast_select_fusion = (bf16[20736,128]{1,0:T(8,128)(2,1)}, bf16[20736,128]{1,0:T(8,128)(2,1)}) fusion(bf16[20736,128]{1,0:T(8,128)(2,1)} %gather_fusion.6, pred[20736]{0:T(1024)(128)(4,1)S(1)} %copy-done.2, bf16[20736,128]{1,0:T(8,128)(2,1)} %gather_fusion.2), kind=kLoop, calls=%fused_computation.7 | loop fusion | flops 5308416 | bytes 21254400 | tf_op jit(solution)/shard_map/jit(_take)/select_n | solution.py:48
  181.5 10.4 %reshape.69 = bf16[768,3456]{1,0:T(8,128)(2,1)} reshape(bf16[20736,128]{1,0:T(8,128)(2,1)} %get-tuple-element.12) | data formatting | bytes 10616832 | tf_op jit(solution)/shard_map/reshape | solution.py:49
  191.9 10.4 %reshape.75 = bf16[768,3456]{1,0:T(8,128)(2,1)} reshape(bf16[20736,128]{1,0:T(8,128)(2,1)} %get-tuple-element.11) | data formatting | bytes 10616832 | tf_op jit(solution)/shard_map/reshape | solution.py:49
  202.3 4.3 %multiply_convert_fusion = (bf16[768,128]{1,0:T(8,128)(2,1)S(1)}, f32[768,128]{1,0:T(8,128)S(1)}) fusion(bf16[768,3456]{1,0:T(8,128)(2,1)} %reshape.69, bf16[3456,128]{1,0:T(8,128)(2,1)} %all_gather.6), kind=kOutput, calls=%fused_computation.20 | convolution fusion | flops 679968768 | bytes 6782976 | tf_op jit(solution)/shard_map/dot_general | solution.py:70
  207.4 2.3 collective-permute-start.2
  209.6 1.5 collective-permute-start.3
  211.1 10.7 %fusion.2 = f32[3456,128]{1,0:T(8,128)} fusion(bf16[768,3456]{1,0:T(8,128)(2,1)} %reshape.69, bf16[768,3456]{1,0:T(8,128)(2,1)} %reshape.75, bf16[3456,128]{1,0:T(8,128)(2,1)S(1)} %bitcast.33, f32[768,128]{1,0:T(8,128)S(1)} %get-tuple-element.18), kind=kOutput, calls=%fused_computation.15 | convolution fusion | flops 1359839232 | bytes 13664256 | tf_op jit(solution)/shard_map/dot_general | solution.py:94
  222.0 42.0 %gather_fusion.4 = bf16[20736,128]{1,0:T(8,128)(2,1)} fusion(bf16[1344,128]{1,0:T(8,128)(2,1)S(1)} %bitcast.31, s32[21504]{0:T(1024)S(1)} %copy-done.1), kind=kCustom, calls=%fused_computation.4.clone | custom fusion | bytes 10699776 | tf_op jit(solution)/shard_map/jit(_take)/gather | solution.py:48
  264.1 13.9 %broadcast_select_fusion.2 = bf16[20736,128]{1,0:T(8,128)(2,1)} fusion(bf16[20736,128]{1,0:T(8,128)(2,1)} %gather_fusion.4, pred[20736]{0:T(1024)(128)(4,1)S(1)} %copy-done.2), kind=kLoop, calls=%fused_computation.9 | loop fusion | flops 2654208 | bytes 10637568 | tf_op jit(solution)/shard_map/jit(_take)/select_n | solution.py:48
  278.0 10.4 %reshape.72 = bf16[768,3456]{1,0:T(8,128)(2,1)} reshape(bf16[20736,128]{1,0:T(8,128)(2,1)} %broadcast_select_fusion.2) | data formatting | bytes 10616832 | tf_op jit(solution)/shard_map/reshape | solution.py:49
  288.4 5.3 %fusion.11 = f32[3456,128]{1,0:T(8,128)} fusion(bf16[768,3456]{1,0:T(8,128)(2,1)} %reshape.72, bf16[768,128]{1,0:T(8,128)(2,1)S(1)} %bitcast.34), kind=kOutput, calls=%fused_computation.41 | convolution fusion | flops 679477248 | bytes 7274496 | tf_op jit(solution)/shard_map/dot_general | solution.py:93
  293.8 4.7 %convolution_convert_fusion = bf16[768,128]{1,0:T(8,128)(2,1)} fusion(bf16[768,3456]{1,0:T(8,128)(2,1)} %reshape.72, bf16[3456,128]{1,0:T(8,128)(2,1)S(1)} %all_gather.7), kind=kOutput, calls=%fused_computation.13 | convolution fusion | flops 679575552 | bytes 6389760 | tf_op jit(solution)/shard_map/dot_general | solution.py:76
  298.5 56.3 %reduce-scatter.9.cloned.1.call-done = f32[216,128]{1,0:T(8,128)} async-done(((f32[3456,128]{1,0:T(8,128)}), f32[216,128]{1,0:T(8,128)}) %reduce-scatter.9.cloned.1.call-update) | async-done | bytes 110608
  (42 shorter events, 4.6 us)
Async XLA Ops:
  7.2 22.1 %copy-start.5 = (s32[64,27]{1,0:T(8,128)S(1)}, s32[64,27]{1,0:T(8,128)}, u32[]{:S(2)}) copy-start(s32[64,27]{1,0:T(8,128)} %constant.22.clone) | copy-start | bytes 20740
  7.2 23.7 %copy-start.3 = (bf16[216,128]{1,0:T(8,128)(2,1)S(1)}, bf16[216,128]{1,0:T(8,128)(2,1)}, u32[]{:S(2)}) copy-start(bf16[216,128]{1,0:T(8,128)(2,1)} %param.18) | copy-start | bytes 165892
  7.2 51.0 %copy-start.4 = (bf16[216,128]{1,0:T(8,128)(2,1)S(1)}, bf16[216,128]{1,0:T(8,128)(2,1)}, u32[]{:S(2)}) copy-start(bf16[216,128]{1,0:T(8,128)(2,1)} %param.19) | copy-start | bytes 165892
  7.2 291.3 %reduce-scatter.7.cloned.1.call-start = ((), (), s32[]{:S(2)}) async-start(), calls=%async_computation.2 | async-start | bytes 1880064
  12.4 67.2 %collective-permute-start = (bf16[4,64,128]{2,1,0:T(8,128)(2,1)}, bf16[4,64,128]{2,1,0:T(8,128)(2,1)}, u32[]{:S(2)}, u32[]{:S(2)}) collective-permute-start(bf16[4,64,128]{2,1,0:T(8,128)(2,1)} %get-tuple-element.9), channel_id=1, source_target_pairs={{0,1},{1,2},{2,3},{3,4},{4,5},{5,6},{6,7},{7,8},{8,9},{9,10},{10,1... | collective-permute-start | bytes 196616 | tf_op jit(solution)/shard_map/ppermute | solution.py:17
  15.4 64.3 %collective-permute-start.1 = (bf16[4,64,128]{2,1,0:T(8,128)(2,1)}, bf16[4,64,128]{2,1,0:T(8,128)(2,1)}, u32[]{:S(2)}, u32[]{:S(2)}) collective-permute-start(bf16[4,64,128]{2,1,0:T(8,128)(2,1)} %get-tuple-element.10), channel_id=1, source_target_pairs={{1,0},{2,1},{3,2},{4,3},{5,4},{6,5},{7,6},{8,7},{9,8},{10,9},{11,1... | collective-permute-start | bytes 196616 | tf_op jit(solution)/shard_map/ppermute | solution.py:18
  17.3 62.3 %collective-permute-start.4 = (bf16[4,64,128]{2,1,0:T(8,128)(2,1)}, bf16[4,64,128]{2,1,0:T(8,128)(2,1)}, u32[]{:S(2)}, u32[]{:S(2)}) collective-permute-start(bf16[4,64,128]{2,1,0:T(8,128)(2,1)} %get-tuple-element.5), channel_id=1, source_target_pairs={{0,1},{1,2},{2,3},{3,4},{4,5},{5,6},{6,7},{7,8},{8,9},{9,10},{10,1... | collective-permute-start | bytes 196616 | tf_op jit(solution)/shard_map/ppermute | solution.py:17
  22.5 57.1 %collective-permute-start.5 = (bf16[4,64,128]{2,1,0:T(8,128)(2,1)}, bf16[4,64,128]{2,1,0:T(8,128)(2,1)}, u32[]{:S(2)}, u32[]{:S(2)}) collective-permute-start(bf16[4,64,128]{2,1,0:T(8,128)(2,1)} %get-tuple-element.6), channel_id=1, source_target_pairs={{1,0},{2,1},{3,2},{4,3},{5,4},{6,5},{7,6},{8,7},{9,8},{10,9},{11,1... | collective-permute-start | bytes 196616 | tf_op jit(solution)/shard_map/ppermute | solution.py:18
  28.5 51.1 %copy-start = (bf16[12,64,128]{2,1,0:T(8,128)(2,1)S(1)}, bf16[12,64,128]{2,1,0:T(8,128)(2,1)}, u32[]{:S(2)}) copy-start(bf16[12,64,128]{2,1,0:T(8,128)(2,1)} %param.20) | copy-start | bytes 589828
  80.8 46.0 %copy-start.1 = (s32[21504]{0:T(1024)S(1)}, s32[21504]{0:T(1024)}, u32[]{:S(2)}) copy-start(s32[21504]{0:T(1024)} %pad_clamp_fusion) | copy-start | bytes 258052
  126.8 42.1 %copy-start.2 = (pred[20736]{0:T(1024)(128)(4,1)S(1)}, pred[20736]{0:T(1024)(128)(4,1)}, u32[]{:S(2)}) copy-start(pred[20736]{0:T(1024)(128)(4,1)} %compare_and_fusion) | copy-start | bytes 62212
  207.4 14.6 %collective-permute-start.2 = (bf16[4,64,128]{2,1,0:T(8,128)(2,1)S(1)}, bf16[4,64,128]{2,1,0:T(8,128)(2,1)S(1)}, u32[]{:S(2)}, u32[]{:S(2)}) collective-permute-start(bf16[4,64,128]{2,1,0:T(8,128)(2,1)S(1)} %get-tuple-element.7), channel_id=1, source_target_pairs={{0,1},{1,2},{2,3},{3,4},{4,5},{5,6},{6,7},{7,8},{8,9},{9,10},{10,1... | collective-permute-start | bytes 196616 | tf_op jit(solution)/shard_map/ppermute | solution.py:17
  209.6 12.3 %collective-permute-start.3 = (bf16[4,64,128]{2,1,0:T(8,128)(2,1)S(1)}, bf16[4,64,128]{2,1,0:T(8,128)(2,1)S(1)}, u32[]{:S(2)}, u32[]{:S(2)}) collective-permute-start(bf16[4,64,128]{2,1,0:T(8,128)(2,1)S(1)} %get-tuple-element.8), channel_id=1, source_target_pairs={{1,0},{2,1},{3,2},{4,3},{5,4},{6,5},{7,6},{8,7},{9,8},{10,9},{11,1... | collective-permute-start | bytes 196616 | tf_op jit(solution)/shard_map/ppermute | solution.py:18
  221.9 132.9 %reduce-scatter.9.cloned.1.call-start = ((), (), s32[]{:S(2)}) async-start(), calls=%async_computation.3 | async-start | bytes 1880064
Sparse Core Ops, SparseCore 0:
  222.0 60.9 reduce-scatter.6
  293.9 60.8 reduce-scatter.8
where the time goes:
time: 365 us; the launch traced here: 362 us
  local copies, waits for them, and re-layouts  173 us (47%)
  waiting for transfers between devices  56.4 us (15%)
  blocking collectives  47.2 us (13%)
  other arithmetic  31.4 us (9%)
  matrix products  25.1 us (7%)
  starting transfers between devices  14.5 us (4%)
  between operations  14.3 us (4%)
    gather x3, local copies, waits for them, and re-layouts, windows(): picked = jnp.take(flat, index.reshape(-1).astype(jnp.int32), axis=0)  130 us
    unnamed x4, waiting for transfers between devices  56.4 us
    reshape x3, local copies, waits for them, and re-layouts, windows(): return picked.reshape(table.shape[0] * vox_count, -1)  31.3 us
    all_gather x1, blocking collectives, on_device(): piece = lax.all_gather(w_first, 'tx', axis=0, tiled=True)  27.3 us
    select_n x3, other arithmetic, windows(): picked = jnp.take(flat, index.reshape(-1).astype(jnp.int32), axis=0)  26.5 us
    all_gather x1, blocking collectives, on_device(): second_whole = lax.all_gather(w_second, 'tx', axis=0, tiled=True)  19.9 us
    dot_general x1, matrix products, on_device(): lax.dot_general(inputs, grad_mid, contract, preferred_element_type=jnp.fl...  10.7 us
    ppermute x3, starting transfers between devices, padded_2(): before = lax.ppermute(last, axis, up)  10.4 us
  transfers between devices with their start and end apart: 8, of which 1 were waited for; matrix products, arithmetic and copies ran while one was open for 27% of the time, Pallas kernels for 0%

commit v1 on v0

--- a/solution.py
+++ b/solution.py
@@ -5,6 +5,30 @@
 from jax.sharding import PartitionSpec as P
 
 BS = 4
+
+
+def wall_load(x_local, along_dim):
+    x_local = jnp.moveaxis(x_local, 0, along_dim)
+    local_part = x_local.shape
+    return x_local.reshape(
+        *local_part[:along_dim],
+        local_part[along_dim] * local_part[along_dim + 1],
+        *local_part[along_dim + 2 :]
+    )
+
+
+def feed_the_weights(matrix, group_axis):
+    extent = lax.axis_size(group_axis)
+    v1 = matrix[None]
+    for num in range(extent.bit_length() - 1):
+        taken_in = 1 << num
+        reached = lax.ppermute(
+            v1, axis_name=group_axis, perm=[(to_i, to_i ^ taken_in) for to_i in range(extent)]
+        )
+        new = jnp.stack([v1, reached], axis=0)
+        b_next = lax.axis_index(group_axis) >> num & 1
+        v1 = jnp.where(b_next == 0, new, new[::-1]).reshape(-1, *matrix.shape)
+    return v1
 
 
 def padded_2(x, sides, width):
@@ -50,6 +74,10 @@
 
 
 def on_device(features, nbr_table, rim_slots, w_first, w_second, cotangent):
+
+    def _point_vectors(vec, inp, out_dim=0):
+        return wall_load(feed_the_weights(vec, inp), out_dim)
+
     capacity, vox_count, channels = features.shape
     rim_count = rim_slots.shape[1] // 2
     brick_code, voxel_code = brick_tables(BS)
@@ -65,7 +93,7 @@
         )
 
     inputs = windows(extend(features), nbr_table, brick_code, voxel_code)
-    piece = lax.all_gather(w_first, "tx", axis=0, tiled=True)
+    piece = _point_vectors(w_first, "tx")
     column_block = lax.slice_in_dim(inputs, 0, piece.shape[0], axis=1)
     first_sum = jnp.dot(column_block, piece, preferred_element_type=jnp.float32)
     hidden = jax.nn.silu(first_sum).astype(jnp.bfloat16)

time: 365 us -> 353 us (0.967)
  blocking collectives: 47.2 us -> 24.3 us
  waiting for transfers between devices: 56.4 us -> 64.1 us
    all_gather x1 -> x0, blocking collectives: 27.3 us -> none  [on_device(): piece = lax.all_gather(w_first, 'tx', axis=0, tiled=True)]
    all_gather x1, blocking collectives: 19.9 us -> 24.3 us  [on_device(): second_whole = lax.all_gather(w_second, 'tx', axis=0, tiled=True)]
    unnamed x4, waiting for transfers between devices: 56.4 us -> 60.3 us
    ppermute x0 -> x4, waiting for transfers between devices: none -> 3.82 us  [feed_the_weights(): lax.ppermute(v1, axis_name=group_axis, perm=[(to_i, to_i ^ taken_in) for...]
  transfers between devices with their start and end apart: 8 -> 12, of which waited for: 1 -> 2; matrix products, arithmetic and copies ran while one was open for 27% -> 63% of each run, Pallas kernels for 0% -> 0%
where the time goes in v1:
time: 353 us; the launch traced here: 350 us
  local copies, waits for them, and re-layouts  174 us (49%)
  waiting for transfers between devices  64.1 us (18%)
  other arithmetic  32.9 us (9%)
  matrix products  24.8 us (7%)
  blocking collectives  24.3 us (7%)
  starting transfers between devices  15.9 us (5%)
  between operations  14.4 us (4%)
    gather x3, local copies, waits for them, and re-layouts, windows(): picked = jnp.take(flat, index.reshape(-1).astype(jnp.int32), axis=0)  130 us
    unnamed x4, waiting for transfers between devices  60.3 us
    reshape x3, local copies, waits for them, and re-layouts, windows(): return picked.reshape(table.shape[0] * vox_count, -1)  31.3 us
    select_n x3, other arithmetic, windows(): picked = jnp.take(flat, index.reshape(-1).astype(jnp.int32), axis=0)  26.6 us
    all_gather x1, blocking collectives, on_device(): second_whole = lax.all_gather(w_second, 'tx', axis=0, tiled=True)  24.3 us
    dot_general x1, matrix products, on_device(): lax.dot_general(inputs, grad_mid, contract, preferred_element_type=jnp.fl...  10.8 us
    ppermute x3, starting transfers between devices, padded_2(): before = lax.ppermute(last, axis, up)  9.43 us
  transfers between devices with their start and end apart: 12, of which 2 were waited for; matrix products, arithmetic and copies ran while one was open for 63% of the time, Pallas kernels for 0%

profile of v1, /device:TPU:0, one launch (start us, length us, event | category | flops | bytes accessed | tf_op | source)
XLA Modules:
  0.0 350.0 jit_solution(15262538560965138177)
XLA Ops:
  8.6 0.9 concatenate.22
  9.5 0.9 concatenate.18
  11.7 0.7 fusion.12
  12.4 3.0 collective-permute-start
  15.4 1.3 collective-permute-start.1
  17.3 5.2 %collective-permute-start.8 = (bf16[4,64,128]{2,1,0:T(8,128)(2,1)}, bf16[4,64,128]{2,1,0:T(8,128)(2,1)}, u32[]{:S(2)}, u32[]{:S(2)}) collective-permute-start(bf16[4,64,128]{2,1,0:T(8,128)(2,1)} %get-tuple-element.5), channel_id=1, source_target_pairs={{0,1},{1,2},{2,3},{3,4},{4,5},{5,6},{6,7},{7,8},{8,9},{9,10},{10,1... | collective-permute-start | bytes 196616 | tf_op jit(solution)/shard_map/ppermute | solution.py:41
  22.5 1.3 collective-permute-start.9
  23.8 1.8 collective-permute-start.2
  25.6 0.8 copy.23
  26.4 0.7 pad_clamp_fusion.1
  27.1 3.3 gather_fusion
  32.1 24.3 %all_gather.3 = bf16[3456,128]{1,0:T(8,128)(2,1)S(1)} all-gather(bf16[216,128]{1,0:T(8,128)(2,1)S(1)} %copy-done.5), channel_id=1, replica_groups=mesh['groups'=2,'tx'=16] {'tx'}, dimensions={0}, use_global_device_ids=true | all-gather | bytes 940032 | tf_op jit(solution)/shard_map/all_gather | solution.py:100
  57.2 1.3 copy.25
  58.6 3.8 %collective-permute-done.3 = bf16[2,216,128]{2,1,0:T(8,128)(2,1)S(1)} collective-permute-done((bf16[2,216,128]{2,1,0:T(8,128)(2,1)S(1)}, bf16[2,216,128]{2,1,0:T(8,128)(2,1)S(1)}, u32[]{:S(2)}, u32[]{:S(2)}) %collective-permute-start.3) | collective-permute-done | bytes 110624 | tf_op jit(solution)/shard_map/ppermute | solution.py:25
  62.7 1.2 maximum_maximum_fusion.2
  63.9 46.0 %gather_fusion.6 = bf16[20736,128]{1,0:T(8,128)(2,1)} fusion(bf16[1344,128]{1,0:T(8,128)(2,1)S(1)} %bitcast.45, s32[21504]{0:T(1024)} %pad_clamp_fusion), kind=kCustom, calls=%fused_computation.5.clone | custom fusion | bytes 10699776 | tf_op jit(solution)/shard_map/jit(_take)/gather | solution.py:72
  109.8 42.1 %gather_fusion.2 = bf16[20736,128]{1,0:T(8,128)(2,1)} fusion(bf16[1344,128]{1,0:T(8,128)(2,1)S(1)} %bitcast.44, s32[21504]{0:T(1024)S(1)} %copy-done.1), kind=kCustom, calls=%fused_computation.1.clone | custom fusion | bytes 10699776 | tf_op jit(solution)/shard_map/jit(_take)/gather | solution.py:72
  151.9 0.7 copy-done.2
  152.6 1.0 pad_maximum_fusion.1
  154.1 12.7 %broadcast_select_fusion = (bf16[20736,128]{1,0:T(8,128)(2,1)}, bf16[20736,128]{1,0:T(8,128)(2,1)}) fusion(bf16[20736,128]{1,0:T(8,128)(2,1)} %gather_fusion.6, pred[20736]{0:T(1024)(128)(4,1)S(1)} %copy-done.3, bf16[20736,128]{1,0:T(8,128)(2,1)} %gather_fusion.2), kind=kLoop, calls=%fused_computation.7 | loop fusion | flops 5308416 | bytes 21254400 | tf_op jit(solution)/shard_map/jit(_take)/select_n | solution.py:72
  166.8 10.4 %reshape.78 = bf16[768,3456]{1,0:T(8,128)(2,1)} reshape(bf16[20736,128]{1,0:T(8,128)(2,1)} %get-tuple-element.14) | data formatting | bytes 10616832 | tf_op jit(solution)/shard_map/reshape | solution.py:73
  177.2 10.5 %reshape.87 = bf16[768,3456]{1,0:T(8,128)(2,1)} reshape(bf16[20736,128]{1,0:T(8,128)(2,1)} %get-tuple-element.13) | data formatting | bytes 10616832 | tf_op jit(solution)/shard_map/reshape | solution.py:73
  188.0 4.1 %multiply_convert_fusion = (bf16[768,128]{1,0:T(8,128)(2,1)S(1)}, f32[768,128]{1,0:T(8,128)S(1)}) fusion(bf16[768,3456]{1,0:T(8,128)(2,1)} %reshape.78, bf16[3456,128]{1,0:T(8,128)(2,1)S(1)} %bitcast.54), kind=kOutput, calls=%fused_computation.24 | convolution fusion | flops 679968768 | bytes 6782976 | tf_op jit(solution)/shard_map/dot_general | solution.py:98
  192.7 1.3 collective-permute-start.6
  194.0 1.5 collective-permute-start.7
  195.5 10.8 %fusion.2 = f32[3456,128]{1,0:T(8,128)} fusion(bf16[768,3456]{1,0:T(8,128)(2,1)} %reshape.78, bf16[768,3456]{1,0:T(8,128)(2,1)} %reshape.87, bf16[3456,128]{1,0:T(8,128)(2,1)S(1)} %bitcast.48, f32[768,128]{1,0:T(8,128)S(1)} %get-tuple-element.20), kind=kOutput, calls=%fused_computation.17 | convolution fusion | flops 1359839232 | bytes 13664256 | tf_op jit(solution)/shard_map/dot_general | solution.py:122
  206.5 42.1 %gather_fusion.4 = bf16[20736,128]{1,0:T(8,128)(2,1)} fusion(bf16[1344,128]{1,0:T(8,128)(2,1)S(1)} %bitcast.46, s32[21504]{0:T(1024)S(1)} %copy-done.1), kind=kCustom, calls=%fused_computation.4.clone | custom fusion | bytes 10699776 | tf_op jit(solution)/shard_map/jit(_take)/gather | solution.py:72
  248.6 13.9 %broadcast_select_fusion.2 = bf16[20736,128]{1,0:T(8,128)(2,1)} fusion(bf16[20736,128]{1,0:T(8,128)(2,1)} %gather_fusion.4, pred[20736]{0:T(1024)(128)(4,1)S(1)} %copy-done.3), kind=kLoop, calls=%fused_computation.9 | loop fusion | flops 2654208 | bytes 10637568 | tf_op jit(solution)/shard_map/jit(_take)/select_n | solution.py:72
  262.5 10.4 %reshape.84 = bf16[768,3456]{1,0:T(8,128)(2,1)} reshape(bf16[20736,128]{1,0:T(8,128)(2,1)} %broadcast_select_fusion.2) | data formatting | bytes 10616832 | tf_op jit(solution)/shard_map/reshape | solution.py:73
  272.9 5.3 %fusion.13 = f32[3456,128]{1,0:T(8,128)} fusion(bf16[768,3456]{1,0:T(8,128)(2,1)} %reshape.84, bf16[768,128]{1,0:T(8,128)(2,1)S(1)} %bitcast.51), kind=kOutput, calls=%fused_computation.51 | convolution fusion | flops 679477248 | bytes 7274496 | tf_op jit(solution)/shard_map/dot_general | solution.py:121
  278.2 4.7 %convolution_convert_fusion = bf16[768,128]{1,0:T(8,128)(2,1)} fusion(bf16[768,3456]{1,0:T(8,128)(2,1)} %reshape.84, bf16[3456,128]{1,0:T(8,128)(2,1)S(1)} %all_gather.3), kind=kOutput, calls=%fused_computation.14 | convolution fusion | flops 679575552 | bytes 6389760 | tf_op jit(solution)/shard_map/dot_general | solution.py:104
  282.9 60.2 %reduce-scatter.9.cloned.1.call-done = f32[216,128]{1,0:T(8,128)} async-done(((f32[3456,128]{1,0:T(8,128)}), f32[216,128]{1,0:T(8,128)}) %reduce-scatter.9.cloned.1.call-update) | async-done | bytes 110608
  (59 shorter events, 7.7 us)
Async XLA Ops:
  7.2 23.9 %copy-start.6 = (s32[64,27]{1,0:T(8,128)S(1)}, s32[64,27]{1,0:T(8,128)}, u32[]{:S(2)}) copy-start(s32[64,27]{1,0:T(8,128)} %constant.26.clone) | copy-start | bytes 20740
  7.2 49.8 %copy-start.4 = (bf16[216,128]{1,0:T(8,128)(2,1)S(1)}, bf16[216,128]{1,0:T(8,128)(2,1)}, u32[]{:S(2)}) copy-start(bf16[216,128]{1,0:T(8,128)(2,1)} %param.18) | copy-start | bytes 165892
  7.2 24.9 %copy-start.5 = (bf16[216,128]{1,0:T(8,128)(2,1)S(1)}, bf16[216,128]{1,0:T(8,128)(2,1)}, u32[]{:S(2)}) copy-start(bf16[216,128]{1,0:T(8,128)(2,1)} %param.19) | copy-start | bytes 165892
  7.2 275.7 %reduce-scatter.7.cloned.1.call-start = ((), (), s32[]{:S(2)}) async-start(), calls=%async_computation.2 | async-start | bytes 1880064
  12.4 50.2 %collective-permute-start = (bf16[4,64,128]{2,1,0:T(8,128)(2,1)}, bf16[4,64,128]{2,1,0:T(8,128)(2,1)}, u32[]{:S(2)}, u32[]{:S(2)}) collective-permute-start(bf16[4,64,128]{2,1,0:T(8,128)(2,1)} %get-tuple-element.9), channel_id=1, source_target_pairs={{0,1},{1,2},{2,3},{3,4},{4,5},{5,6},{6,7},{7,8},{8,9},{9,10},{10,1... | collective-permute-start | bytes 196616 | tf_op jit(solution)/shard_map/ppermute | solution.py:41
  15.4 47.3 %collective-permute-start.1 = (bf16[4,64,128]{2,1,0:T(8,128)(2,1)}, bf16[4,64,128]{2,1,0:T(8,128)(2,1)}, u32[]{:S(2)}, u32[]{:S(2)}) collective-permute-start(bf16[4,64,128]{2,1,0:T(8,128)(2,1)} %get-tuple-element.10), channel_id=1, source_target_pairs={{1,0},{2,1},{3,2},{4,3},{5,4},{6,5},{7,6},{8,7},{9,8},{10,9},{11,1... | collective-permute-start | bytes 196616 | tf_op jit(solution)/shard_map/ppermute | solution.py:42
  17.3 45.3 %collective-permute-start.8 = (bf16[4,64,128]{2,1,0:T(8,128)(2,1)}, bf16[4,64,128]{2,1,0:T(8,128)(2,1)}, u32[]{:S(2)}, u32[]{:S(2)}) collective-permute-start(bf16[4,64,128]{2,1,0:T(8,128)(2,1)} %get-tuple-element.5), channel_id=1, source_target_pairs={{0,1},{1,2},{2,3},{3,4},{4,5},{5,6},{6,7},{7,8},{8,9},{9,10},{10,1... | collective-permute-start | bytes 196616 | tf_op jit(solution)/shard_map/ppermute | solution.py:41
  22.5 40.2 %collective-permute-start.9 = (bf16[4,64,128]{2,1,0:T(8,128)(2,1)}, bf16[4,64,128]{2,1,0:T(8,128)(2,1)}, u32[]{:S(2)}, u32[]{:S(2)}) collective-permute-start(bf16[4,64,128]{2,1,0:T(8,128)(2,1)} %get-tuple-element.6), channel_id=1, source_target_pairs={{1,0},{2,1},{3,2},{4,3},{5,4},{6,5},{7,6},{8,7},{9,8},{10,9},{11,1... | collective-permute-start | bytes 196616 | tf_op jit(solution)/shard_map/ppermute | solution.py:42
  23.8 33.2 %collective-permute-start.2 = (bf16[1,216,128]{2,1,0:T(8,128)(2,1)}, bf16[1,216,128]{2,1,0:T(8,128)(2,1)S(1)}, u32[]{:S(2)}, u32[]{:S(2)}) collective-permute-start(bf16[1,216,128]{2,1,0:T(8,128)(2,1)} %bitcast.60), channel_id=1, source_target_pairs={{0,1},{1,0},{2,3},{3,2},{4,5},{5,4},{6,7},{7,6},{8,9},{9,8},{10,11... | collective-permute-start | bytes 165896 | tf_op jit(solution)/shard_map/ppermute | solution.py:25
  30.4 32.3 %copy-start = (bf16[12,64,128]{2,1,0:T(8,128)(2,1)S(1)}, bf16[12,64,128]{2,1,0:T(8,128)(2,1)}, u32[]{:S(2)}) copy-start(bf16[12,64,128]{2,1,0:T(8,128)(2,1)} %param.20) | copy-start | bytes 589828
  57.1 5.4 %collective-permute-start.3 = (bf16[2,216,128]{2,1,0:T(8,128)(2,1)S(1)}, bf16[2,216,128]{2,1,0:T(8,128)(2,1)S(1)}, u32[]{:S(2)}, u32[]{:S(2)}) collective-permute-start(bf16[2,216,128]{2,1,0:T(8,128)(2,1)S(1)} %get-tuple-element.12), channel_id=1, source_target_pairs={{0,2},{1,3},{2,0},{3,1},{4,6},{5,7},{6,4},{7,5},{8,10},{9,11},{10,... | collective-permute-start | bytes 331784 | tf_op jit(solution)/shard_map/ppermute | solution.py:25
  62.5 89.4 %collective-permute-start.4 = (bf16[4,216,128]{2,1,0:T(8,128)(2,1)S(1)}, bf16[4,216,128]{2,1,0:T(8,128)(2,1)S(1)}, u32[]{:S(2)}, u32[]{:S(2)}) collective-permute-start(bf16[4,216,128]{2,1,0:T(8,128)(2,1)S(1)} %bitcast.52), channel_id=1, source_target_pairs={{0,4},{1,5},{2,6},{3,7},{4,0},{5,1},{6,2},{7,3},{8,12},{9,13},{10,... | collective-permute-start | bytes 663560 | tf_op jit(solution)/shard_map/ppermute | solution.py:25
  63.9 46.0 %copy-start.1 = (s32[21504]{0:T(1024)S(1)}, s32[21504]{0:T(1024)}, u32[]{:S(2)}) copy-start(s32[21504]{0:T(1024)} %pad_clamp_fusion) | copy-start | bytes 258052
  109.8 44.3 %copy-start.3 = (pred[20736]{0:T(1024)(128)(4,1)S(1)}, pred[20736]{0:T(1024)(128)(4,1)}, u32[]{:S(2)}) copy-start(pred[20736]{0:T(1024)(128)(4,1)} %compare_and_fusion) | copy-start | bytes 62212
  151.9 0.7 copy-start.2
  153.7 34.0 %collective-permute-start.5 = (bf16[8,216,128]{2,1,0:T(8,128)(2,1)S(1)}, bf16[8,216,128]{2,1,0:T(8,128)(2,1)S(1)}, u32[]{:S(2)}, u32[]{:S(2)}) collective-permute-start(bf16[8,216,128]{2,1,0:T(8,128)(2,1)S(1)} %bitcast.49), channel_id=1, source_target_pairs={{0,8},{1,9},{2,10},{3,11},{4,12},{5,13},{6,14},{7,15},{8,0},{9,1},... | collective-permute-start | bytes 1327112 | tf_op jit(solution)/shard_map/ppermute | solution.py:25
  192.7 13.6 %collective-permute-start.6 = (bf16[4,64,128]{2,1,0:T(8,128)(2,1)S(1)}, bf16[4,64,128]{2,1,0:T(8,128)(2,1)S(1)}, u32[]{:S(2)}, u32[]{:S(2)}) collective-permute-start(bf16[4,64,128]{2,1,0:T(8,128)(2,1)S(1)} %get-tuple-element.7), channel_id=1, source_target_pairs={{0,1},{1,2},{2,3},{3,4},{4,5},{5,6},{6,7},{7,8},{8,9},{9,10},{10,1... | collective-permute-start | bytes 196616 | tf_op jit(solution)/shard_map/ppermute | solution.py:41
  194.0 12.3 %collective-permute-start.7 = (bf16[4,64,128]{2,1,0:T(8,128)(2,1)S(1)}, bf16[4,64,128]{2,1,0:T(8,128)(2,1)S(1)}, u32[]{:S(2)}, u32[]{:S(2)}) collective-permute-start(bf16[4,64,128]{2,1,0:T(8,128)(2,1)S(1)} %get-tuple-element.8), channel_id=1, source_target_pairs={{1,0},{2,1},{3,2},{4,3},{5,4},{6,5},{7,6},{8,7},{9,8},{10,9},{11,1... | collective-permute-start | bytes 196616 | tf_op jit(solution)/shard_map/ppermute | solution.py:42
  206.3 136.9 %reduce-scatter.9.cloned.1.call-start = ((), (), s32[]{:S(2)}) async-start(), calls=%async_computation.3 | async-start | bytes 1880064
Sparse Core Ops, SparseCore 0:
  206.4 64.7 reduce-scatter.6
  278.3 64.7 reduce-scatter.8
